TPU v7x, 32 devices: a whole 2x2x4 slice. The times are simulated.
32 devices in a mesh: groups: 2 (over y), pair: 16 (over z, x, core).
Axes of the slice: x: 2, y: 2, z: 4, core: 2. Of those that a mesh axis runs over, the one named last changes fastest.
Arguments:
- amplitudes: bfloat16 [2048, 8, 4096], P(('groups', 'pair')), parts along dimension 0, may hold values from -6 to 6
- screen: int32 [2048, 8], P(('groups', 'pair')), parts along dimension 0, may hold values from 0 to 15, all different within a row; in each aligned block of 64 rows (0 to 63, 64 to 127, ...) at most 48 rows name the same one
- owner: int32 [32], P('groups'), parts along dimension 0, may hold values from 0 to 15, each once
- factors: bfloat16 [32, 2, 8, 64, 64], P(('groups', 'pair')), parts along dimension 0, may hold values from -0.4375 to 0.4375
- cycle_self: bfloat16 [2048, 64], P(('groups', 'pair')), parts along dimension 0, may hold values from -3 to 3
- cycle_prev: bfloat16 [2048, 64], P(('groups', 'pair')), parts along dimension 0, may hold values from -3 to 3
Outputs:
- residual: bfloat16 [2048, 8, 4096], P(('groups', 'pair')), parts along dimension 0
There are 2 independent parts, one for each index of `groups`. A program takes and returns all parts, laid end to end along the dimension named above; each array names one. Nothing has to cross between parts.
Inputs may be any that keep to these rules, and one draw needn't show every extreme that they name: `screen`: each row names 8 different virtual-pair tiles. In each aligned block of 64 rows (one occupied-pair tile) no tile is named by more than 48 rows, a bound that some block reaches. A permutation: the factors of virtual-pair tile q are row owner[q] of factors.
All inputs are finite; a program needn't handle non-finite values.
Results may differ from a plain program's by a relative error of at most 0.0032.
Values may be sent and summed in bfloat16 or wider, within the bound.
A program may use at most 512 MiB of HBM per device.

v0:
```python
import jax
import jax.numpy as jnp
from jax import lax
from jax.sharding import PartitionSpec as P


def shifted(value, axis, steps):
    count = lax.axis_size(axis)
    first, last = (max(0, -steps), min(count, count - steps))
    return lax.ppermute(value, axis, [(source, source + steps) for source in range(first, last)])


def cycle_term(coupling, first_ids, second_ids, second_items, listed):
    spread = jnp.repeat(jnp.repeat(coupling, listed, 0), listed, 1)
    weights = jnp.where(first_ids[:, None] == second_ids[None, :], spread, jnp.zeros_like(spread))
    return jnp.dot(weights, second_items, preferred_element_type=jnp.float32)


def shards(amplitudes, screen, owner, factors, cycle_self, cycle_prev):
    pair_rows, listed, width = amplitudes.shape
    tile_width = factors.shape[3]
    tile_count = owner.shape[0]
    item_count = pair_rows * listed
    devices = lax.axis_size("pair")
    most = max(2, 3 * pair_rows * listed // (2 * tile_count))
    items = amplitudes.reshape(item_count, width)
    tile_ids = screen.reshape(item_count)
    earlier, earlier_ids = shifted((amplitudes, screen), "pair", 1)
    cycle = cycle_term(cycle_self, tile_ids, tile_ids, items, listed)
    cycle = cycle + cycle_term(
        cycle_prev,
        tile_ids,
        earlier_ids.reshape(item_count),
        earlier.reshape(item_count, width),
        listed,
    )
    table_hit = tile_ids[:, None] == jnp.arange(tile_count, dtype=jnp.int32)[None, :]
    holders = jnp.sum(jnp.where(table_hit, owner[None, :], 0), axis=1)
    hot = (holders[:, None] == jnp.arange(devices, dtype=jnp.int32)[None, :]).astype(jnp.int32)
    before = jnp.cumsum(hot, axis=0) - hot
    position = holders * most + jnp.sum(before * hot, axis=1)
    inverse = (
        jnp.full((devices * most,), item_count, jnp.int32)
        .at[position]
        .set(jnp.arange(item_count, dtype=jnp.int32))
    )
    padded = jnp.concatenate([items, jnp.zeros((1, width), items.dtype)], axis=0)
    everything = lax.all_gather(factors, "pair", axis=0, tiled=True)
    slotted = padded[inverse].reshape(devices, most, tile_width, tile_width)
    total = jnp.zeros((devices, most, tile_width, tile_width), jnp.float32)
    for index in range(factors.shape[2]):
        half = jnp.einsum(
            "qac,qmcd->qmad", everything[:, 0, index], slotted, preferred_element_type=jnp.float32
        ).astype(jnp.bfloat16)
        total = total + jnp.einsum(
            "qmad,qbd->qmab", half, everything[:, 1, index], preferred_element_type=jnp.float32
        )
    ladder = total.astype(jnp.bfloat16).reshape(devices * most, width)[position]
    residual = (ladder.astype(jnp.float32) + cycle).astype(jnp.bfloat16)
    return residual.reshape(pair_rows, listed, width)


def solution(mesh):
    placed = (
        P(("groups", "pair"), None, None),
        P(("groups", "pair"), None),
        P("groups"),
        P(("groups", "pair"), None, None, None, None),
        P(("groups", "pair"), None),
        P(("groups", "pair"), None),
    )
    return jax.shard_map(
        shards,
        mesh=mesh,
        in_specs=placed,
        out_specs=P(("groups", "pair"), None, None),
        check_vma=False,
    )
```

profile of v0, /device:TPU:0, one launch (start us, length us, event | category | flops | bytes accessed | tf_op | source)
XLA Modules:
  0.0 296.3 jit_solution(13896697519404260383)
XLA Ops:
  6.5 0.0 copy-start
  6.5 0.0 all-gather.2.cloned.1.call-start
  6.5 0.7 all-gather.2.cloned.1.call-update
  7.3 6.5 %copy.16 = bf16[64,8,4096]{2,0,1:T(8,128)(2,1)} copy(bf16[64,8,4096]{2,1,0:T(8,128)(2,1)} %param.6) | data formatting | bytes 8388608 | tf_op args[0]
  13.8 4.3 %collective-permute-start.1 = (bf16[64,8,4096]{2,0,1:T(8,128)(2,1)}, bf16[64,8,4096]{2,0,1:T(8,128)(2,1)}, u32[]{:S(2)}, u32[]{:S(2)}) collective-permute-start(bf16[64,8,4096]{2,0,1:T(8,128)(2,1)} %copy.16), channel_id=1, source_target_pairs={{0,1},{1,2},{2,3},{3,4},{4,5},{5,6},{6,7},{7,8},{8,9},{9,10},{10,1... | collective-permute-start | bytes 12582920 | tf_op jit(solution)/shard_map/ppermute | solution.py:10
  18.1 3.1 %collective-permute-start = (s32[64,8]{0,1:T(8,128)}, s32[64,8]{0,1:T(8,128)}, u32[]{:S(2)}, u32[]{:S(2)}) collective-permute-start(s32[64,8]{0,1:T(8,128)} %param.7), channel_id=1, source_target_pairs={{0,1},{1,2},{2,3},{3,4},{4,5},{5,6},{6,7},{7,8},{8,9},{9,10},{10,1... | collective-permute-start | bytes 6152 | tf_op jit(solution)/shard_map/ppermute | solution.py:10
  21.2 0.8 copy.12
  22.0 0.1 eq.64
  22.1 0.0 copy-start.5
  22.1 0.7 select_reduce_fusion
  22.8 1.1 reduce-window.6
  24.0 0.2 slice_reduce_fusion
  24.3 4.8 %concatenate.3 = bf16[513,4096]{1,0:T(8,128)(2,1)} pad(bf16[512,4096]{1,0:T(8,128)(2,1)} %bitcast.215, bf16[]{:T(256)} %constant.6.clone.1), padding=0_1x0_0 | pad | bytes 8396802 | tf_op jit(solution)/shard_map/concatenate | solution.py:47
  29.1 0.1 fusion.54
  29.2 2.6 scatter_custom_fusion
  31.8 14.7 %gather_fusion = bf16[768,4096]{1,0:T(8,128)(2,1)} fusion(bf16[513,4096]{1,0:T(8,128)(2,1)} %concatenate.3, s32[1024]{0:T(1024)S(1)} %pad_clamp_fusion.1), kind=kCustom, calls=%fused_computation | custom fusion | bytes 12585984 | tf_op jit(solution)/shard_map/gather | solution.py:49
  46.6 0.0 copy-start.3
  46.6 0.0 copy-start.7
  46.6 18.0 %reshape.91 = bf16[16,48,64,64]{3,2,1,0:T(8,128)(2,1)} reshape(bf16[768,4096]{1,0:T(8,128)(2,1)} %gather_fusion) | data formatting | bytes 12582912 | tf_op jit(solution)/shard_map/reshape | solution.py:49
  64.5 0.0 copy-done
  64.6 0.1 copy.15
  64.7 0.0 copy-done.3
  64.7 0.7 copy.17
  65.4 0.6 pad_clamp_fusion
  66.0 0.0 copy-done.5
  66.0 0.0 copy-done.7
  66.0 11.1 %fusion.43 = f32[512,4096,1]{1,0,2:T(8,128)} fusion(s32[64,8]{0,1:T(8,128)S(1)} %copy-done.7, s32[512]{0:T(512)S(1)} %eq.64, bf16[512,64]{0,1:T(8,128)(2,1)S(1)} %copy.15, bf16[64,8,4096]{2,1,0:T(8,128)(2,1)} %param.6), kind=kOutput, calls=%fused_computation.42 | convolution fusion | flops 2148007936 | bytes 12652544 | tf_op jit(solution)/shard_map/dot_general | solution.py:16
  77.1 0.0 all-gather.2.cloned.1.call-done
  77.1 15.8 %fusion.10 = f32[16,48,64,64]{3,2,1,0:T(8,128)} fusion(bf16[16,48,64,64]{3,2,1,0:T(8,128)(2,1)} %reshape.91, bf16[16,2,8,64,64]{4,3,0,2,1:T(8,128)(2,1)} %all-gather.2.cloned.1.call-done), kind=kOutput, calls=%fused_computation.14 | convolution fusion | flops 808452096 | bytes 25690112 | tf_op jit(solution)/shard_map/qmad,qbd->qmab/dot_general | solution.py:55
  92.9 15.7 %fusion.12 = f32[16,48,64,64]{3,2,1,0:T(8,128)} fusion(bf16[16,48,64,64]{3,2,1,0:T(8,128)(2,1)} %reshape.91, bf16[16,2,8,64,64]{4,3,0,2,1:T(8,128)(2,1)} %all-gather.2.cloned.1.call-done), kind=kOutput, calls=%fused_computation.16 | convolution fusion | flops 808452096 | bytes 25690112 | tf_op jit(solution)/shard_map/qmad,qbd->qmab/dot_general | solution.py:55
  108.7 15.6 %fusion.14 = f32[16,48,64,64]{3,2,1,0:T(8,128)} fusion(bf16[16,48,64,64]{3,2,1,0:T(8,128)(2,1)} %reshape.91, bf16[16,2,8,64,64]{4,3,0,2,1:T(8,128)(2,1)} %all-gather.2.cloned.1.call-done), kind=kOutput, calls=%fused_computation.18 | convolution fusion | flops 808452096 | bytes 25690112 | tf_op jit(solution)/shard_map/qmad,qbd->qmab/dot_general | solution.py:55
  124.2 15.7 %fusion.2 = f32[16,48,64,64]{3,2,1,0:T(8,128)} fusion(bf16[16,48,64,64]{3,2,1,0:T(8,128)(2,1)} %reshape.91, bf16[16,2,8,64,64]{4,3,0,2,1:T(8,128)(2,1)} %all-gather.2.cloned.1.call-done), kind=kOutput, calls=%fused_computation.6 | convolution fusion | flops 808452096 | bytes 25690112 | tf_op jit(solution)/shard_map/qmad,qbd->qmab/dot_general | solution.py:55
  139.9 15.9 %fusion.4 = f32[16,48,64,64]{3,2,1,0:T(8,128)} fusion(bf16[16,48,64,64]{3,2,1,0:T(8,128)(2,1)} %reshape.91, bf16[16,2,8,64,64]{4,3,0,2,1:T(8,128)(2,1)} %all-gather.2.cloned.1.call-done), kind=kOutput, calls=%fused_computation.8 | convolution fusion | flops 808452096 | bytes 25690112 | tf_op jit(solution)/shard_map/qmad,qbd->qmab/dot_general | solution.py:55
  155.9 15.7 %fusion.6 = f32[16,48,64,64]{3,2,1,0:T(8,128)} fusion(bf16[16,48,64,64]{3,2,1,0:T(8,128)(2,1)} %reshape.91, bf16[16,2,8,64,64]{4,3,0,2,1:T(8,128)(2,1)} %all-gather.2.cloned.1.call-done), kind=kOutput, calls=%fused_computation.10 | convolution fusion | flops 808452096 | bytes 25690112 | tf_op jit(solution)/shard_map/qmad,qbd->qmab/dot_general | solution.py:55
  171.5 15.6 %fusion.8 = f32[16,48,64,64]{3,2,1,0:T(8,128)} fusion(bf16[16,48,64,64]{3,2,1,0:T(8,128)(2,1)} %reshape.91, bf16[16,2,8,64,64]{4,3,0,2,1:T(8,128)(2,1)} %all-gather.2.cloned.1.call-done), kind=kOutput, calls=%fused_computation.12 | convolution fusion | flops 808452096 | bytes 25690112 | tf_op jit(solution)/shard_map/qmad,qbd->qmab/dot_general | solution.py:55
  187.1 62.0 %add_convert_fusion = bf16[16,48,64,64]{3,2,1,0:T(8,128)(2,1)} fusion(f32[16,48,64,64]{3,2,1,0:T(8,128)} %fusion.2, f32[16,48,64,64]{3,2,1,0:T(8,128)} %fusion.4, f32[16,48,64,64]{3,2,1,0:T(8,128)} %fusion.6, f32[16,48,64,64]{3,2,1,0:T(8,128)} %fusion.8, f32[16,48,64,64]{3,2,1,0:T(8,128)} %fusion.10, f32[16,48,64,64]{3,2,1,0:T(8,128)} %fusion.14, ...), kind=kOutput, calls=%fused_computation.3 | convolution fusion | flops 833617920 | bytes 195559424 | tf_op jit(solution)/shard_map/qmad,qbd->qmab/dot_general | solution.py:55
  249.1 0.0 copy-start.4
  249.1 17.0 %reshape.92 = bf16[768,4096]{1,0:T(8,128)(2,1)} reshape(bf16[16,48,64,64]{3,2,1,0:T(8,128)(2,1)} %add_convert_fusion) | data formatting | bytes 12582912 | tf_op jit(solution)/shard_map/reshape | solution.py:58
  266.1 0.0 copy-done.4
  266.1 0.0 copy-start.2
  266.1 0.0 copy-start.6
  266.1 12.4 %gather_fusion.1 = bf16[512,4096]{1,0:T(8,128)(2,1)} fusion(bf16[768,4096]{1,0:T(8,128)(2,1)} %reshape.92, s32[1024]{0:T(1024)S(1)} %copy-done.4), kind=kCustom, calls=%fused_computation.1 | custom fusion | bytes 8390656 | tf_op jit(solution)/shard_map/gather | solution.py:58
  278.5 0.0 collective-permute-done
  278.5 0.0 collective-permute-done.1
  278.6 0.0 copy-done.2
  278.6 0.0 copy-done.6
  278.6 0.0 copy-start.1
  278.6 10.7 %fusion.42 = bf16[64,8,4096]{2,1,0:T(8,128)(2,1)} fusion(bf16[64,8,4096]{2,0,1:T(8,128)(2,1)} %collective-permute-done.1, f32[512,4096,1]{1,0,2:T(8,128)} %fusion.43, bf16[512,4096]{1,0:T(8,128)(2,1)} %gather_fusion.1, s32[64,8]{0,1:T(8,128)} %collective-permute-done, s32[512]{0:T(512)S(1)} %copy-done.6, bf16[512,64]{0,1:T(8,128)(2,1)S(1)} %copy-done.2), kind=kOutput, calls=%fused_computation.39 | convolution fusion | flops 2156396544 | bytes 21041152 | tf_op jit(solution)/shard_map/dot_general | solution.py:16
  289.2 0.0 copy-done.1
  (10 shorter events, 0.1 us)
Async XLA Ops:
  6.5 58.0 %copy-start = (bf16[64,64]{1,0:T(8,128)(2,1)S(1)}, bf16[64,64]{1,0:T(8,128)(2,1)}, u32[]{:S(2)}) copy-start(bf16[64,64]{1,0:T(8,128)(2,1)} %param.10) | copy-start | bytes 24580
  6.5 70.6 %all-gather.2.cloned.1.call-start = ((), (), s32[]{:S(2)}) async-start(), calls=%async_computation | async-start | bytes 4456448 | tf_op jit(solution)/shard_map/all_gather | solution.py:48
  13.8 264.8 %collective-permute-start.1 = (bf16[64,8,4096]{2,0,1:T(8,128)(2,1)}, bf16[64,8,4096]{2,0,1:T(8,128)(2,1)}, u32[]{:S(2)}, u32[]{:S(2)}) collective-permute-start(bf16[64,8,4096]{2,0,1:T(8,128)(2,1)} %copy.16), channel_id=1, source_target_pairs={{0,1},{1,2},{2,3},{3,4},{4,5},{5,6},{6,7},{7,8},{8,9},{9,10},{10,1... | collective-permute-start | bytes 12582920 | tf_op jit(solution)/shard_map/ppermute | solution.py:10
  18.1 260.5 %collective-permute-start = (s32[64,8]{0,1:T(8,128)}, s32[64,8]{0,1:T(8,128)}, u32[]{:S(2)}, u32[]{:S(2)}) collective-permute-start(s32[64,8]{0,1:T(8,128)} %param.7), channel_id=1, source_target_pairs={{0,1},{1,2},{2,3},{3,4},{4,5},{5,6},{6,7},{7,8},{8,9},{9,10},{10,1... | collective-permute-start | bytes 6152 | tf_op jit(solution)/shard_map/ppermute | solution.py:10
  22.1 43.9 %copy-start.5 = (s32[512]{0:T(512)}, s32[512]{0:T(512)S(1)}, u32[]{:S(2)}) copy-start(s32[512]{0:T(512)S(1)} %eq.64) | copy-start | bytes 6148
  46.6 18.1 %copy-start.3 = (bf16[64,64]{1,0:T(8,128)(2,1)S(1)}, bf16[64,64]{1,0:T(8,128)(2,1)}, u32[]{:S(2)}) copy-start(bf16[64,64]{1,0:T(8,128)(2,1)} %param.11) | copy-start | bytes 24580
  46.6 19.5 %copy-start.7 = (s32[64,8]{0,1:T(8,128)S(1)}, s32[64,8]{0,1:T(8,128)}, u32[]{:S(2)}) copy-start(s32[64,8]{0,1:T(8,128)} %param.7) | copy-start | bytes 6148
  249.1 17.0 %copy-start.4 = (s32[1024]{0:T(1024)S(1)}, s32[1024]{0:T(1024)}, u32[]{:S(2)}) copy-start(s32[1024]{0:T(1024)} %pad_clamp_fusion) | copy-start | bytes 12292
  266.1 12.5 %copy-start.2 = (bf16[512,64]{0,1:T(8,128)(2,1)S(1)}, bf16[512,64]{0,1:T(8,128)(2,1)}, u32[]{:S(2)}) copy-start(bf16[512,64]{0,1:T(8,128)(2,1)} %copy.17) | copy-start | bytes 196612
  266.1 12.5 %copy-start.6 = (s32[512]{0:T(512)S(1)}, s32[512]{0:T(512)}, u32[]{:S(2)}) copy-start(s32[512]{0:T(512)} %copy-done.5) | copy-start | bytes 6148
  278.6 10.7 %copy-start.1 = (bf16[64,64]{1,0:T(8,128)(2,1)S(1)}, bf16[64,64]{1,0:T(8,128)(2,1)}, u32[]{:S(2)}) copy-start(bf16[64,64]{1,0:T(8,128)(2,1)} %param.10) | copy-start | bytes 24580
Sparse Core Ops, SparseCore 0:
  9.5 59.9 all-gather.1
where the time goes:
time: 301 us; the launch traced here: 296 us
  matrix products  194 us (64%)
  local copies, waits for them, and re-layouts  78.1 us (26%)
  between operations  13.7 us (5%)
  starting transfers between devices  7.46 us (2%)
    dot_general x8, matrix products, shards(): jnp.einsum('qmad,qbd->qmab', half, everything[:, 1, index], preferred_ele...  172 us
    dot_general x2, matrix products, cycle_term(): return jnp.dot(weights, second_items, preferred_element_type=jnp.float32)  21.8 us
    reshape x1, local copies, waits for them, and re-layouts, shards(): slotted = padded[inverse].reshape(devices, most, tile_width, tile_width)  18 us
    reshape x1, local copies, waits for them, and re-layouts, shards(): ladder = total.astype(jnp.bfloat16).reshape(devices * most, width)[position]  17 us
    gather x1, local copies, waits for them, and re-layouts, shards(): slotted = padded[inverse].reshape(devices, most, tile_width, tile_width)  14.7 us
    gather x1, local copies, waits for them, and re-layouts, shards(): ladder = total.astype(jnp.bfloat16).reshape(devices * most, width)[position]  12.4 us
    ppermute x2, starting transfers between devices, shifted(): lax.ppermute(value, axis, [(source, source + steps) for source in range(f...  7.46 us
    unnamed x18, local copies, waits for them, and re-layouts  7.31 us
  transfers between devices with their start and end apart: 3, of which 0 were waited for; matrix products, arithmetic and copies ran while one was open for 89% of the time, Pallas kernels for 0%

commit v1 on v0

v1 whole, which is shorter than its diff:
```python
import functools

import jax
import jax.numpy as jnp
from jax import lax
from jax.experimental import pallas as pl
from jax.experimental.pallas import tpu as pltpu
from jax.sharding import PartitionSpec as P

BF, F32 = jnp.bfloat16, jnp.float32


def shifted(value, axis, steps):
    count = lax.axis_size(axis)
    first, last = (max(0, -steps), min(count, count - steps))
    return lax.ppermute(value, axis, [(source, source + steps) for source in range(first, last)])


def spread_weights(coupling, first_ids, second_ids, listed):
    spread = jnp.repeat(jnp.repeat(coupling, listed, 0), listed, 1)
    return jnp.where(first_ids[:, None] == second_ids[None, :], spread, jnp.zeros_like(spread))


def ladder_kernel(
    tiles, chunks, most, vt, naux,
    owner_ref, slot_row_ref, slot_col_ref, x_ref, w_ref, f_ref,
    out_ref, g_ref, l_ref, z_ref, xt_ref, h_ref, b_ref, o_ref,
):
    step = pl.program_id(0)
    half_rows = most // 2
    pieces = vt // 2
    quads = most // 4
    items = x_ref.shape[0]
    slots = tiles * most
    lane = lax.broadcasted_iota(jnp.int32, (half_rows, 128), 1)
    low = lane < 64
    width = x_ref.shape[1]

    @pl.when(step == 0)
    def _():
        xt_ref[...] = jnp.zeros_like(xt_ref)

    @pl.when(step < chunks)
    def _():
        place = lax.broadcasted_iota(jnp.int32, (slots, items), 0)
        hot = jnp.where(place == slot_row_ref[...], 1.0, 0.0).astype(BF)
        picked = jnp.dot(hot, x_ref[...], preferred_element_type=F32)
        g_ref[:, pl.ds(pl.multiple_of(step * width, width), width)] = picked.astype(BF)

    @pl.when(jnp.logical_and(step >= chunks, step < chunks + tiles))
    def _():
        base = pl.multiple_of((step - chunks) * most, most)
        factor = f_ref[0]
        row = lax.broadcasted_iota(jnp.int32, (2 * vt, 4 * vt), 0)
        col = lax.broadcasted_iota(jnp.int32, (2 * vt, 4 * vt), 1)
        copies = jnp.where(row == vt + col % vt, 1.0, 0.0).astype(BF)
        tiled = jnp.dot(factor, copies, preferred_element_type=F32)
        part = lax.broadcasted_iota(jnp.int32, (vt, 4 * vt), 1) // vt
        for g in range(naux):
            for mi in range(4):
                b_ref[(g * 4 + mi) * vt : (g * 4 + mi + 1) * vt, :] = jnp.where(
                    part == mi, tiled[g * vt : (g + 1) * vt, :], 0.0
                ).astype(BF)
        for j in range(pieces):
            both = g_ref[pl.ds(base, most), j * 128 : (j + 1) * 128].astype(F32)
            first, second = both[:half_rows], both[half_rows:]
            z_ref[j * half_rows : (j + 1) * half_rows, :] = jnp.where(
                low, first, pltpu.roll(second, 64, 1)
            )
            z_ref[(pieces + j) * half_rows : (pieces + j + 1) * half_rows, :] = jnp.where(
                low, pltpu.roll(first, 64, 1), second
            )
        for m in range(half_rows):
            xt_ref[0:vt, m * 128 : (m + 1) * 128] = z_ref[pl.ds(m, vt, stride=half_rows), :].astype(BF)
        for k in range(quads):
            half = jnp.dot(factor, xt_ref[:, k * 256 : (k + 1) * 256], preferred_element_type=F32)
            half = half.astype(BF)
            for g in range(naux):
                h_ref[k * vt : (k + 1) * vt, g * 256 : (g + 1) * 256] = half[g * vt : (g + 1) * vt, :]
        result = jnp.dot(h_ref[...], b_ref[...], preferred_element_type=F32)
        for k in range(quads):
            for side in range(2):
                m = 2 * k + side
                o_ref[m * vt : (m + 1) * vt, :] = result[
                    k * vt : (k + 1) * vt, side * 128 : (side + 1) * 128
                ]
        for j in range(pieces):
            even = o_ref[pl.ds(j, half_rows, stride=vt), :]
            odd = o_ref[pl.ds(pieces + j, half_rows, stride=vt), :]
            first = jnp.where(low, even, pltpu.roll(odd, 64, 1))
            second = jnp.where(low, pltpu.roll(even, 64, 1), odd)
            l_ref[pl.ds(base, most), j * 128 : (j + 1) * 128] = jnp.concatenate(
                [first, second], 0
            ).astype(BF)

    @pl.when(step >= chunks + tiles)
    def _():
        at = pl.multiple_of((step - chunks - tiles) * width, width)
        place = lax.broadcasted_iota(jnp.int32, (items, slots), 1)
        hot = jnp.where(place == slot_col_ref[...], 1.0, 0.0).astype(BF)
        ladder = jnp.dot(hot, l_ref[:, pl.ds(at, width)], preferred_element_type=F32)
        out_ref[...] = ladder + jnp.dot(w_ref[...], x_ref[...], preferred_element_type=F32)


def last_kernel(part_ref, w_ref, x_ref, out_ref):
    out_ref[...] = (
        part_ref[...] + jnp.dot(w_ref[...], x_ref[...], preferred_element_type=F32)
    ).astype(BF)


def shards(amplitudes, screen, owner, factors, cycle_self, cycle_prev):
    pair_rows, listed, width = amplitudes.shape
    naux, vt = factors.shape[2], factors.shape[3]
    tiles = owner.shape[0]
    items = pair_rows * listed
    most = max(2, 3 * items // (2 * tiles))
    most = -(-most // 16) * 16
    slots = tiles * most
    chunks, wide = 8, width // 8
    x = amplitudes.reshape(items, width)
    ids = screen.reshape(items)
    earlier, earlier_ids = shifted((amplitudes, screen), "pair", 1)

    left = factors[:, 0].reshape(1, naux, vt // 2, 2, vt // 2, 2)
    left = left.transpose(0, 1, 3, 2, 5, 4).reshape(1, naux * vt, vt)
    right = factors[:, 1].transpose(0, 1, 3, 2).reshape(1, naux * vt, vt)
    packed = jnp.concatenate([left, right], 2)
    everything = lax.all_gather(packed, "pair", axis=0, tiled=True)

    same = ids[:, None] == ids[None, :]
    order = jnp.arange(items, dtype=jnp.int32)
    ahead = jnp.where(same & (order[:, None] < order[None, :]), 1, 0)
    slot = ids * most + jnp.sum(ahead, axis=0, dtype=jnp.int32)
    own_weights = spread_weights(cycle_self, ids, ids, listed)

    def x_at(s, *_):
        return (0, jnp.where(s < chunks, s, jnp.maximum(s - chunks - tiles, 0)))

    partial = pl.pallas_call(
        functools.partial(ladder_kernel, tiles, chunks, most, vt, naux),
        out_shape=jax.ShapeDtypeStruct((items, width), F32),
        grid_spec=pltpu.PrefetchScalarGridSpec(
            num_scalar_prefetch=1,
            grid=(chunks + tiles + chunks,),
            in_specs=[
                pl.BlockSpec((1, items), lambda s, o: (0, 0)),
                pl.BlockSpec((items, 1), lambda s, o: (0, 0)),
                pl.BlockSpec((items, wide), x_at),
                pl.BlockSpec((items, items), lambda s, o: (0, 0)),
                pl.BlockSpec(
                    (1, naux * vt, 2 * vt),
                    lambda s, o: (o[jnp.clip(s - chunks, 0, tiles - 1)], 0, 0),
                ),
            ],
            out_specs=pl.BlockSpec(
                (items, wide), lambda s, o: (0, jnp.maximum(s - chunks - tiles, 0))
            ),
            scratch_shapes=[
                pltpu.VMEM((slots, width), BF),
                pltpu.VMEM((slots, width), BF),
                pltpu.VMEM((vt * most // 2, 128), F32),
                pltpu.VMEM((2 * vt, most * vt), BF),
                pltpu.VMEM((most // 4 * vt, naux * 256), BF),
                pltpu.VMEM((naux * 256, 256), BF),
                pltpu.VMEM((vt * most // 2, 128), F32),
            ],
        ),
        compiler_params=pltpu.CompilerParams(vmem_limit_bytes=56 * 2**20),
        cost_estimate=pl.CostEstimate(
            flops=60 * 10**9, bytes_accessed=20 * 2**20, transcendentals=0
        ),
        name="ladder",
    )(owner, slot[None, :], slot[:, None], x, own_weights, everything)

    earlier_weights = spread_weights(cycle_prev, ids, earlier_ids.reshape(items), listed)
    residual = pl.pallas_call(
        last_kernel,
        out_shape=jax.ShapeDtypeStruct((items, width), BF),
        grid=(chunks,),
        in_specs=[
            pl.BlockSpec((items, wide), lambda s: (0, s)),
            pl.BlockSpec((items, items), lambda s: (0, 0)),
            pl.BlockSpec((items, wide), lambda s: (0, s)),
        ],
        out_specs=pl.BlockSpec((items, wide), lambda s: (0, s)),
        compiler_params=pltpu.CompilerParams(vmem_limit_bytes=32 * 2**20),
        name="cycle",
    )(partial, earlier_weights, earlier.reshape(items, width))
    return residual.reshape(pair_rows, listed, width)


def solution(mesh):
    placed = (
        P(("groups", "pair"), None, None),
        P(("groups", "pair"), None),
        P("groups"),
        P(("groups", "pair"), None, None, None, None),
        P(("groups", "pair"), None),
        P(("groups", "pair"), None),
    )
    return jax.shard_map(
        shards,
        mesh=mesh,
        in_specs=placed,
        out_specs=P(("groups", "pair"), None, None),
        check_vma=False,
    )
```

time: 301 us -> 139 us (0.46); the launches traced: 296 us -> 138 us
  matrix products: 194 us -> 0 us
  Pallas kernels: 0 us -> 69.9 us
  local copies, waits for them, and re-layouts: 78.1 us -> 9.77 us
  waiting for transfers between devices: 0.72 us -> 34 us
    dot_general x10 -> x0, matrix products: 194 us -> none  [the longest x8 172 us: shards(): jnp.einsum('qmad,qbd->qmab', half, everything[:, 1, index], preferred_ele...]
    pallas_call x0 -> x2, Pallas kernels: none -> 69.9 us  [the longest x1 61.7 us: shards(): pl.pallas_call(functools.partial(ladder_kernel, tiles, chunks, most, vt,...]
    reshape x6 -> x10, local copies, waits for them, and re-layouts: 35.9 us -> 1.15 us  [the longest x8 0.78 us: spread_weights(): spread = jnp.repeat(jnp.repeat(coupling, listed, 0), listed, 1)]
    all_gather x1, waiting for transfers between devices: 0.01 us -> 34 us  [shards(): everything = lax.all_gather(packed, 'pair', axis=0, tiled=True)]
    gather x2 -> x0, local copies, waits for them, and re-layouts: 27.2 us -> none  [the longest x1 14.7 us: shards(): slotted = padded[inverse].reshape(devices, most, tile_width, tile_width)]
    concatenate x1, local copies, waits for them, and re-layouts: 4.8 us -> 0.76 us  [shards(): packed = jnp.concatenate([left, right], 2)]
    unnamed x18 -> x9, local copies, waits for them, and re-layouts: 7.31 us -> 3.47 us
  transfers between devices with their start and end apart: 3 -> 3, of which waited for: 0 -> 1; matrix products, arithmetic and copies ran while one was open for 89% -> 3% of each run, Pallas kernels for 0% -> 45%
where the time goes in v1:
time: 139 us; the launch traced here: 138 us
  Pallas kernels  69.9 us (50%)
  waiting for transfers between devices  34 us (24%)
  between operations  13.5 us (10%)
  local copies, waits for them, and re-layouts  9.77 us (7%)
  starting transfers between devices  8.84 us (6%)
  other arithmetic  1.93 us (1%)
    pallas_call x1, Pallas kernels, shards(): pl.pallas_call(functools.partial(ladder_kernel, tiles, chunks, most, vt,...  61.7 us
    all_gather x1, waiting for transfers between devices, shards(): everything = lax.all_gather(packed, 'pair', axis=0, tiled=True)  34 us
    ppermute x2, starting transfers between devices, shifted(): lax.ppermute(value, axis, [(source, source + steps) for source in range(f...  8.84 us
    pallas_call x1, Pallas kernels, shards(): pl.pallas_call(last_kernel, out_shape=jax.ShapeDtypeStruct((items, width)...  8.16 us
    unnamed x9, local copies, waits for them, and re-layouts  3.47 us
  transfers between devices with their start and end apart: 3, of which 1 were waited for; matrix products, arithmetic and copies ran while one was open for 3% of the time, Pallas kernels for 45%

profile of v1, /device:TPU:0, one launch (start us, length us, event | category | flops | bytes accessed | tf_op | source)
XLA Modules:
  0.0 137.9 jit_solution(4194547323580938883)
XLA Ops:
  6.5 0.0 copy-start
  6.5 0.0 copy-start.3
  6.5 0.0 copy-start.2
  6.5 0.0 all-gather.2.cloned.1.call-start
  6.5 1.0 fusion
  7.6 0.1 copy.60
  7.7 0.1 reshape.73
  7.8 0.5 copy.58
  8.3 1.4 %copy.59 = bf16[1,8,2,32,2,32]{3,2,1,5,4,0:T(2,128)(2,1)S(1)} copy(bf16[1,8,2,32,2,32]{1,4,5,2,3,0:T(2,128)(2,1)S(1)} %bitcast.26) | data formatting | bytes 131072 | tf_op jit(solution)/shard_map/transpose | solution.py:125
  9.7 0.2 reshape.72
  9.9 0.8 copy.61
  10.7 0.0 all-gather.2.cloned.1.call-update
  10.7 0.0 copy-done.3
  10.7 2.4 %collective-permute-start = (s32[64,8]{0,1:T(8,128)S(1)}, s32[64,8]{0,1:T(8,128)S(1)}, u32[]{:S(2)}, u32[]{:S(2)}) collective-permute-start(s32[64,8]{0,1:T(8,128)S(1)} %copy-done.3), channel_id=1, source_target_pairs={{0,1},{1,2},{2,3},{3,4},{4,5},{5,6},{6,7},{7,8},{8,9},{9,10},{10,1... | collective-permute-start | bytes 6152 | tf_op jit(solution)/shard_map/ppermute | solution.py:16
  13.1 6.5 %collective-permute-start.1 = (bf16[64,8,4096]{2,1,0:T(8,128)(2,1)}, bf16[64,8,4096]{2,1,0:T(8,128)(2,1)}, u32[]{:S(2)}, u32[]{:S(2)}) collective-permute-start(bf16[64,8,4096]{2,1,0:T(8,128)(2,1)} %param.6), channel_id=1, source_target_pairs={{0,1},{1,2},{2,3},{3,4},{4,5},{5,6},{6,7},{7,8},{8,9},{9,10},{10,1... | collective-permute-start | bytes 12582920 | tf_op jit(solution)/shard_map/ppermute | solution.py:16
  19.6 0.1 copy.54
  19.7 0.1 eq.14
  19.7 0.0 copy-done
  19.8 0.1 copy.56
  19.9 0.0 copy-done.2
  19.9 0.1 copy.64
  20.0 0.1 broadcast_bitcast_fusion
  20.1 0.1 broadcast_bitcast_fusion.1
  20.2 0.2 select_reduce_fusion
  20.4 0.1 copy.53
  20.5 0.1 mul.29
  20.5 0.1 mul.28
  20.7 0.9 copy.62.slot_col_ref
  21.5 0.2 copy.65
  21.7 0.2 copy.57
  22.0 0.6 add.19.slot_row_ref
  22.6 0.0 collective-permute-done
  22.6 0.1 copy.63
  22.7 0.1 eq.18
  22.7 1.1 compare_select_fusion.1
  23.9 34.0 %all-gather.2.cloned.1.call-done.f_ref = bf16[16,512,128]{2,1,0:T(8,128)(2,1)} async-done(((bf16[1,512,128]{2,1,0:T(8,128)(2,1)}), bf16[16,512,128]{2,1,0:T(8,128)(2,1)}) %all-gather.2.cloned.1.call-update) | async-done | bytes 2097168 | tf_op jit(solution)/shard_map/all_gather | solution.py:128
  57.8 61.7 %ladder.1.part_ref = f32[512,4096]{1,0:T(8,128)} custom-call(s32[16]{0:T(128)} %owner_ref.1, s32[1,512]{1,0:T(1,128)} %add.19.slot_row_ref, s32[512,1]{1,0:T(8,128)} %copy.62.slot_col_ref, bf16[512,4096]{1,0:T(8,128)(2,1)} %bitcast.29, bf16[512,512]{1,0:T(8,128)(2,1)} %get-tuple-element.8.w_ref, bf16[16,512,128]{2,1,0:T(8,128)(2,1)} %all-gather.2.cloned.1.call-done.f_ref), custom_call_target="tpu_custom_call" | custom-call | flops 60000002048 | bytes 20971520 | tf_op jit(solution)/shard_map/ladder/pallas_call | solution.py:139
  119.5 0.0 collective-permute-done.1
  119.5 0.0 copy-start.1
  119.5 3.4 %copy-done.1 = f32[512,4096]{1,0:T(8,128)S(1)} copy-done((f32[512,4096]{1,0:T(8,128)S(1)}, f32[512,4096]{1,0:T(8,128)}, u32[]{:S(2)}) %copy-start.1) | copy-done | bytes 8388632
  122.9 8.2 %cycle.1 = bf16[512,4096]{1,0:T(8,128)(2,1)} custom-call(f32[512,4096]{1,0:T(8,128)S(1)} %copy-done.1, bf16[512,512]{1,0:T(8,128)(2,1)S(1)} %get-tuple-element.7.w_ref, bf16[512,4096]{1,0:T(8,128)(2,1)} %bitcast.11.x_ref), custom_call_target="tpu_custom_call" | custom-call | tf_op jit(solution)/shard_map/cycle/pallas_call | solution.py:176
  (5 shorter events, 0.1 us)
Async XLA Ops:
  6.5 13.2 %copy-start = (bf16[64,64]{1,0:T(8,128)(2,1)S(1)}, bf16[64,64]{1,0:T(8,128)(2,1)}, u32[]{:S(2)}) copy-start(bf16[64,64]{1,0:T(8,128)(2,1)} %param.10) | copy-start | bytes 24580
  6.5 4.2 %copy-start.3 = (s32[64,8]{0,1:T(8,128)S(1)}, s32[64,8]{0,1:T(8,128)}, u32[]{:S(2)}) copy-start(s32[64,8]{0,1:T(8,128)} %param.7) | copy-start | bytes 6148
  6.5 13.3 %copy-start.2 = (bf16[64,64]{1,0:T(8,128)(2,1)S(1)}, bf16[64,64]{1,0:T(8,128)(2,1)}, u32[]{:S(2)}) copy-start(bf16[64,64]{1,0:T(8,128)(2,1)} %param.11) | copy-start | bytes 24580
  6.5 51.3 %all-gather.2.cloned.1.call-start = ((), (), s32[]{:S(2)}) async-start(), calls=%async_computation | async-start | bytes 2228224 | tf_op jit(solution)/shard_map/all_gather | solution.py:128
  10.7 11.8 %collective-permute-start = (s32[64,8]{0,1:T(8,128)S(1)}, s32[64,8]{0,1:T(8,128)S(1)}, u32[]{:S(2)}, u32[]{:S(2)}) collective-permute-start(s32[64,8]{0,1:T(8,128)S(1)} %copy-done.3), channel_id=1, source_target_pairs={{0,1},{1,2},{2,3},{3,4},{4,5},{5,6},{6,7},{7,8},{8,9},{9,10},{10,1... | collective-permute-start | bytes 6152 | tf_op jit(solution)/shard_map/ppermute | solution.py:16
  13.1 106.4 %collective-permute-start.1 = (bf16[64,8,4096]{2,1,0:T(8,128)(2,1)}, bf16[64,8,4096]{2,1,0:T(8,128)(2,1)}, u32[]{:S(2)}, u32[]{:S(2)}) collective-permute-start(bf16[64,8,4096]{2,1,0:T(8,128)(2,1)} %param.6), channel_id=1, source_target_pairs={{0,1},{1,2},{2,3},{3,4},{4,5},{5,6},{6,7},{7,8},{8,9},{9,10},{10,1... | collective-permute-start | bytes 12582920 | tf_op jit(solution)/shard_map/ppermute | solution.py:16
  119.5 3.4 %copy-start.1 = (f32[512,4096]{1,0:T(8,128)S(1)}, f32[512,4096]{1,0:T(8,128)}, u32[]{:S(2)}) copy-start(f32[512,4096]{1,0:T(8,128)} %ladder.1.part_ref) | copy-start | bytes 25165828
Sparse Core Ops, SparseCore 0:
  10.8 46.9 all-gather.1

commit v2 on v1

v2 whole, which is shorter than its diff:
```python
import functools

import jax
import jax.numpy as jnp
from jax import lax
from jax.experimental import pallas as pl
from jax.experimental.pallas import tpu as pltpu
from jax.sharding import PartitionSpec as P

BF, F32 = jnp.bfloat16, jnp.float32


def shifted(value, axis, steps):
    count = lax.axis_size(axis)
    first, last = (max(0, -steps), min(count, count - steps))
    return lax.ppermute(value, axis, [(source, source + steps) for source in range(first, last)])


def spread_weights(coupling, first_ids, second_ids, listed):
    spread = jnp.repeat(jnp.repeat(coupling, listed, 0), listed, 1)
    return jnp.where(first_ids[:, None] == second_ids[None, :], spread, jnp.zeros_like(spread))


def spread_kernel(
    chunks, most, vt, slot_row_ref, x_ref, xt_ref, g_ref, z_ref, hot_ref
):
    step = pl.program_id(0)
    half_rows = most // 2
    pieces = vt // 2
    slots, items = hot_ref.shape
    width = x_ref.shape[1]
    low = lax.broadcasted_iota(jnp.int32, (half_rows, 128), 1) < 64

    @pl.when(step == 0)
    def _():
        place = lax.broadcasted_iota(jnp.int32, (slots, items), 0)
        hot_ref[...] = jnp.where(place == slot_row_ref[...], 1.0, 0.0).astype(BF)

    @pl.when(step < chunks)
    def _():
        picked = jnp.dot(hot_ref[...], x_ref[...], preferred_element_type=F32)
        g_ref[:, pl.ds(pl.multiple_of(step * width, width), width)] = picked.astype(BF)

    @pl.when(step >= chunks)
    def _():
        base = pl.multiple_of((step - chunks) * most, most)
        for j in range(pieces):
            both = g_ref[pl.ds(base, most), j * 128 : (j + 1) * 128].astype(F32)
            first, second = both[:half_rows], both[half_rows:]
            z_ref[j * half_rows : (j + 1) * half_rows, :] = jnp.where(
                low, first, pltpu.roll(second, 64, 1)
            )
            z_ref[(pieces + j) * half_rows : (pieces + j + 1) * half_rows, :] = jnp.where(
                low, pltpu.roll(first, 64, 1), second
            )
        for m in range(half_rows):
            xt_ref[0, :, m * 128 : (m + 1) * 128] = z_ref[
                pl.ds(m, vt, stride=half_rows), :
            ].astype(BF)


def ladder_kernel(
    most, vt, naux, owner_ref, count_ref, f_ref, xt_ref, l_ref, h_ref, b_ref, o_ref
):
    half_rows = most // 2
    pieces = vt // 2
    quads = most // 4
    pitch = vt + 8
    low = lax.broadcasted_iota(jnp.int32, (half_rows, 128), 1) < 64
    count = count_ref[pl.program_id(0)]
    row = lax.broadcasted_iota(jnp.int32, (2 * vt, 4 * vt), 0)
    col = lax.broadcasted_iota(jnp.int32, (2 * vt, 4 * vt), 1)
    copies = jnp.where(row == vt + col % vt, 1.0, 0.0).astype(BF)
    tiled = jnp.dot(f_ref[0], copies, preferred_element_type=F32)
    part = lax.broadcasted_iota(jnp.int32, (vt, 4 * vt), 1) // vt
    for g in range(naux):
        for mi in range(4):
            b_ref[(g * 4 + mi) * vt : (g * 4 + mi + 1) * vt, :] = jnp.where(
                part == mi, tiled[g * vt : (g + 1) * vt, :], 0.0
            ).astype(BF)

    def run(used):
        left = f_ref[0, :, :vt]
        for k in range(used):
            half = jnp.dot(
                left, xt_ref[0, :, k * 256 : (k + 1) * 256], preferred_element_type=F32
            ).astype(BF)
            for g in range(naux):
                h_ref[k * vt : (k + 1) * vt, g * 256 : (g + 1) * 256] = half[
                    g * vt : (g + 1) * vt, :
                ]
        result = jnp.dot(h_ref[: used * vt, :], b_ref[...], preferred_element_type=F32)
        for k in range(used):
            for side in range(2):
                m = 2 * k + side
                o_ref[m * pitch : m * pitch + vt, :] = result[
                    k * vt : (k + 1) * vt, side * 128 : (side + 1) * 128
                ]
        if used < quads:
            o_ref[2 * used * pitch :, :] = jnp.zeros((2 * (quads - used) * pitch, 128), F32)

    unit = quads // 4
    for turn in range(4):
        least = turn * unit * 4
        most_here = least + unit * 4
        fits = count <= most_here
        if turn > 0:
            fits = jnp.logical_and(fits, count > least)
        pl.when(fits)(functools.partial(run, (turn + 1) * unit))

    for j in range(pieces):
        even = o_ref[pl.ds(j, half_rows, stride=pitch), :]
        odd = o_ref[pl.ds(pieces + j, half_rows, stride=pitch), :]
        first = jnp.where(low, even, pltpu.roll(odd, 64, 1))
        second = jnp.where(low, pltpu.roll(even, 64, 1), odd)
        l_ref[:, j * 128 : (j + 1) * 128] = jnp.concatenate([first, second], 0).astype(BF)


def own_kernel(w_ref, x_ref, out_ref):
    out_ref[...] = jnp.dot(w_ref[...], x_ref[...], preferred_element_type=F32)


def last_kernel(slot_col_ref, l_ref, part_ref, v_ref, e_ref, out_ref, hot_ref):
    @pl.when(pl.program_id(0) == 0)
    def _():
        place = lax.broadcasted_iota(jnp.int32, hot_ref.shape, 1)
        hot_ref[...] = jnp.where(place == slot_col_ref[...], 1.0, 0.0).astype(BF)

    total = jnp.dot(hot_ref[...], l_ref[...], preferred_element_type=F32)
    total += part_ref[...]
    total += jnp.dot(v_ref[...], e_ref[...], preferred_element_type=F32)
    out_ref[...] = total.astype(BF)


def shards(amplitudes, screen, owner, factors, cycle_self, cycle_prev):
    pair_rows, listed, width = amplitudes.shape
    naux, vt = factors.shape[2], factors.shape[3]
    tiles = owner.shape[0]
    items = pair_rows * listed
    most = max(2, 3 * items // (2 * tiles))
    most = -(-most // 16) * 16
    slots = tiles * most
    chunks, wide = 8, width // 8
    x = amplitudes.reshape(items, width)
    ids = screen.reshape(items)
    earlier_ids = shifted(screen, "pair", 1)

    left = factors[:, 0].reshape(1, naux, vt // 2, 2, vt // 2, 2)
    left = left.transpose(0, 1, 3, 2, 5, 4).reshape(1, naux * vt, vt)
    right = factors[:, 1].transpose(0, 1, 3, 2).reshape(1, naux * vt, vt)
    packed = jnp.concatenate([left, right], 2)
    everything = lax.all_gather(packed, "pair", axis=0, tiled=True)

    same = ids[:, None] == ids[None, :]
    order = jnp.arange(items, dtype=jnp.int32)
    ahead = jnp.where(same & (order[:, None] < order[None, :]), 1, 0)
    rank = jnp.sum(ahead, axis=0, dtype=jnp.int32)
    slot = ids * most + rank % 2 * (most // 2) + rank // 2
    named = ids[:, None] == jnp.arange(tiles, dtype=jnp.int32)[None, :]
    count = jnp.sum(named, axis=0, dtype=jnp.int32)
    own_weights = spread_weights(cycle_self, ids, ids, listed)

    columns = pl.pallas_call(
        functools.partial(spread_kernel, chunks, most, vt),
        out_shape=jax.ShapeDtypeStruct((tiles, vt, most * vt), BF),
        grid=(chunks + tiles,),
        in_specs=[
            pl.BlockSpec((1, items), lambda s: (0, 0)),
            pl.BlockSpec((items, wide), lambda s: (0, jnp.minimum(s, chunks - 1))),
        ],
        out_specs=pl.BlockSpec(
            (1, vt, most * vt), lambda s: (jnp.maximum(s - chunks, 0), 0, 0)
        ),
        scratch_shapes=[
            pltpu.VMEM((slots, width), BF),
            pltpu.VMEM((vt * most // 2, 128), F32),
            pltpu.VMEM((slots, items), BF),
        ],
        compiler_params=pltpu.CompilerParams(vmem_limit_bytes=56 * 2**20),
        cost_estimate=pl.CostEstimate(
            flops=25 * 10**9, bytes_accessed=10 * 2**20, transcendentals=0
        ),
        name="spread",
    )(slot[None, :], x)

    own = pl.pallas_call(
        own_kernel,
        out_shape=jax.ShapeDtypeStruct((items, width), F32),
        grid=(chunks,),
        in_specs=[
            pl.BlockSpec((items, items), lambda s: (0, 0)),
            pl.BlockSpec((items, wide), lambda s: (0, s)),
        ],
        out_specs=pl.BlockSpec((items, wide), lambda s: (0, s)),
        compiler_params=pltpu.CompilerParams(vmem_limit_bytes=56 * 2**20),
        cost_estimate=pl.CostEstimate(
            flops=3 * 10**9, bytes_accessed=12 * 2**20, transcendentals=0
        ),
        name="own",
    )(own_weights, x)

    held, columns, own = lax.optimization_barrier((amplitudes, columns, own))
    earlier = shifted(held, "pair", 1)
    ladder = pl.pallas_call(
        functools.partial(ladder_kernel, most, vt, naux),
        out_shape=jax.ShapeDtypeStruct((slots, width), BF),
        grid_spec=pltpu.PrefetchScalarGridSpec(
            num_scalar_prefetch=2,
            grid=(tiles,),
            in_specs=[
                pl.BlockSpec((1, naux * vt, 2 * vt), lambda s, o, n: (o[s], 0, 0)),
                pl.BlockSpec((1, vt, most * vt), lambda s, o, n: (s, 0, 0)),
            ],
            out_specs=pl.BlockSpec((most, width), lambda s, o, n: (s, 0)),
            scratch_shapes=[
                pltpu.VMEM((most // 4 * vt, naux * 256), BF),
                pltpu.VMEM((naux * 256, 256), BF),
                pltpu.VMEM(((vt + 8) * most // 2, 128), F32),
            ],
        ),
        compiler_params=pltpu.CompilerParams(vmem_limit_bytes=56 * 2**20),
        cost_estimate=pl.CostEstimate(
            flops=40 * 10**9, bytes_accessed=14 * 2**20, transcendentals=0
        ),
        name="ladder",
    )(owner, count, everything, columns)

    earlier_weights = spread_weights(cycle_prev, ids, earlier_ids.reshape(items), listed)
    residual = pl.pallas_call(
        last_kernel,
        out_shape=jax.ShapeDtypeStruct((items, width), BF),
        grid=(chunks,),
        in_specs=[
            pl.BlockSpec((items, 1), lambda s: (0, 0)),
            pl.BlockSpec((slots, wide), lambda s: (0, s)),
            pl.BlockSpec((items, wide), lambda s: (0, s)),
            pl.BlockSpec((items, items), lambda s: (0, 0)),
            pl.BlockSpec((items, wide), lambda s: (0, s)),
        ],
        out_specs=pl.BlockSpec((items, wide), lambda s: (0, s)),
        scratch_shapes=[pltpu.VMEM((items, slots), BF)],
        compiler_params=pltpu.CompilerParams(vmem_limit_bytes=56 * 2**20),
        cost_estimate=pl.CostEstimate(
            flops=8 * 10**9, bytes_accessed=18 * 2**20, transcendentals=0
        ),
        name="cycle",
    )(slot[:, None], ladder, own, earlier_weights, earlier.reshape(items, width))
    return residual.reshape(pair_rows, listed, width)


def solution(mesh):
    placed = (
        P(("groups", "pair"), None, None),
        P(("groups", "pair"), None),
        P("groups"),
        P(("groups", "pair"), None, None, None, None),
        P(("groups", "pair"), None),
        P(("groups", "pair"), None),
    )
    return jax.shard_map(
        shards,
        mesh=mesh,
        in_specs=placed,
        out_specs=P(("groups", "pair"), None, None),
        check_vma=False,
    )
```

time: 139 us -> 117 us (0.84)
  waiting for transfers between devices: 34 us -> 7.11 us
  Pallas kernels: 69.9 us -> 75.7 us
  local copies, waits for them, and re-layouts: 9.77 us -> 5.66 us
  other arithmetic: 1.93 us -> 3.69 us
    all_gather x1, waiting for transfers between devices: 34 us -> 7.09 us  [shards(): everything = lax.all_gather(packed, 'pair', axis=0, tiled=True)]
    pallas_call x1, Pallas kernels: 8.16 us -> 13.4 us  [shards(): pl.pallas_call(last_kernel, out_shape=jax.ShapeDtypeStruct((items, width)...]
    unnamed x9 -> x7, local copies, waits for them, and re-layouts: 3.47 us -> 0.1 us
    pallas_call x1 -> x3, Pallas kernels: 61.7 us -> 62.4 us  [the longest x1 37.2 us: shards(): pl.pallas_call(functools.partial(ladder_kernel, most, vt, naux), out_shap...]
  transfers between devices with their start and end apart: 3 -> 3, of which waited for: 1 -> 1; matrix products, arithmetic and copies ran while one was open for 3% -> 8% of each run, Pallas kernels for 45% -> 54%
where the time goes in v2:
time: 117 us; the launch traced here: 115 us
  Pallas kernels  75.7 us (65%)
  between operations  13.5 us (12%)
  starting transfers between devices  8.98 us (8%)
  waiting for transfers between devices  7.11 us (6%)
  local copies, waits for them, and re-layouts  5.66 us (5%)
  other arithmetic  3.69 us (3%)
    pallas_call x1, Pallas kernels, shards(): pl.pallas_call(functools.partial(ladder_kernel, most, vt, naux), out_shap...  37.2 us
    pallas_call x1, Pallas kernels, shards(): pl.pallas_call(functools.partial(spread_kernel, chunks, most, vt), out_sh...  16.2 us
    pallas_call x1, Pallas kernels, shards(): pl.pallas_call(last_kernel, out_shape=jax.ShapeDtypeStruct((items, width)...  13.4 us
    pallas_call x1, Pallas kernels, shards(): pl.pallas_call(own_kernel, out_shape=jax.ShapeDtypeStruct((items, width),...  9 us
    ppermute x2, starting transfers between devices, shifted(): lax.ppermute(value, axis, [(source, source + steps) for source in range(f...  8.97 us
    all_gather x1, waiting for transfers between devices, shards(): everything = lax.all_gather(packed, 'pair', axis=0, tiled=True)  7.09 us
  transfers between devices with their start and end apart: 3, of which 1 were waited for; matrix products, arithmetic and copies ran while one was open for 8% of the time, Pallas kernels for 54%

profile of v2, /device:TPU:0, one launch (start us, length us, event | category | flops | bytes accessed | tf_op | source)
XLA Modules:
  0.0 114.7 jit_solution(840291142855749936)
XLA Ops:
  6.5 0.0 copy-start
  6.5 0.0 copy-start.2
  6.5 0.0 copy-start.1
  6.5 0.0 all-gather.2.cloned.1.call-start
  6.5 2.5 %collective-permute-start = (s32[64,8]{0,1:T(8,128)}, s32[64,8]{0,1:T(8,128)S(1)}, u32[]{:S(2)}, u32[]{:S(2)}) collective-permute-start(s32[64,8]{0,1:T(8,128)} %param.7), channel_id=1, source_target_pairs={{0,1},{1,2},{2,3},{3,4},{4,5},{5,6},{6,7},{7,8},{8,9},{9,10},{10,1... | collective-permute-start | bytes 6152 | tf_op jit(solution)/shard_map/ppermute | solution.py:16
  9.0 1.0 fusion.10
  10.0 0.5 copy.87
  10.5 1.4 %copy.88 = bf16[1,8,2,32,2,32]{3,2,1,5,4,0:T(2,128)(2,1)S(1)} copy(bf16[1,8,2,32,2,32]{1,4,5,2,3,0:T(2,128)(2,1)S(1)} %bitcast.26) | data formatting | bytes 131072 | tf_op jit(solution)/shard_map/transpose | solution.py:149
  11.9 0.2 reshape.209
  12.1 0.1 copy.89
  12.2 0.1 reshape.210
  12.4 0.8 copy.90
  13.2 0.0 all-gather.2.cloned.1.call-update
  13.2 0.0 copy-done.2
  13.2 0.1 copy.80
  13.3 0.1 eq.22
  13.4 0.2 select_reduce_fusion
  13.6 0.1 copy.79
  13.7 0.1 mul.55
  13.8 0.0 copy-done
  13.8 0.0 copy-done.1
  13.8 0.6 fusion.9.slot_row_ref
  14.4 0.1 copy.92
  14.5 0.1 copy.95
  14.6 0.1 broadcast_bitcast_fusion.1
  14.7 16.2 %spread.1.xt_ref = bf16[16,64,3072]{2,1,0:T(8,128)(2,1)} custom-call(s32[1,512]{1,0:T(1,128)} %fusion.9.slot_row_ref, bf16[512,4096]{1,0:T(8,128)(2,1)} %bitcast.6.x_ref), custom_call_target="tpu_custom_call" | custom-call | flops 24999999488 | bytes 10485760 | tf_op jit(solution)/shard_map/spread/pallas_call | solution.py:163
  30.9 0.1 broadcast_bitcast_fusion
  31.0 0.2 copy.93
  31.2 0.2 copy.96
  31.4 0.0 collective-permute-done
  31.4 0.1 copy.94
  31.5 0.1 eq.29
  31.6 1.3 %compare_select_fusion.1 = (bf16[512,512]{1,0:T(8,128)(2,1)}, bf16[512,512]{1,0:T(8,128)(2,1)}) fusion(bf16[512,512]{1,0:T(8,128)(2,1)S(1)} %copy.96, s32[512]{0:T(512)S(1)} %eq.29, s32[512]{0:T(512)S(1)} %eq.22, bf16[512,512]{1,0:T(8,128)(2,1)S(1)} %copy.93), kind=kLoop, calls=%fused_computation.4 | loop fusion | flops 1048576 | bytes 2101248 | tf_op jit(solution)/shard_map/jit(_where)/select_n | solution.py:21
  32.9 9.0 %own.1.part_ref = f32[512,4096]{1,0:T(8,128)} custom-call(bf16[512,512]{1,0:T(8,128)(2,1)} %get-tuple-element.14.w_ref, bf16[512,4096]{1,0:T(8,128)(2,1)} %bitcast.6.x_ref), custom_call_target="tpu_custom_call" | custom-call | flops 3000000000 | bytes 12582912 | tf_op jit(solution)/shard_map/own/pallas_call | solution.py:186
  41.9 6.5 %collective-permute-start.1 = (bf16[64,8,4096]{2,1,0:T(8,128)(2,1)}, bf16[64,8,4096]{2,1,0:T(8,128)(2,1)}, u32[]{:S(2)}, u32[]{:S(2)}) collective-permute-start(bf16[64,8,4096]{2,1,0:T(8,128)(2,1)} %param.6), channel_id=1, source_target_pairs={{0,1},{1,2},{2,3},{3,4},{4,5},{5,6},{6,7},{7,8},{8,9},{9,10},{10,1... | collective-permute-start | bytes 12582920 | tf_op jit(solution)/shard_map/ppermute | solution.py:16
  48.4 0.1 mul.58
  48.5 0.1 copy.81
  48.6 0.6 convert_reduce_fusion.count_ref
  49.3 1.0 fusion.2.slot_col_ref
  50.2 7.1 %all-gather.2.cloned.1.call-done.f_ref = bf16[16,512,128]{2,1,0:T(8,128)(2,1)} async-done(((bf16[1,512,128]{2,1,0:T(8,128)(2,1)}), bf16[16,512,128]{2,1,0:T(8,128)(2,1)}) %all-gather.2.cloned.1.call-update) | async-done | bytes 2097168 | tf_op jit(solution)/shard_map/all_gather | solution.py:152
  57.3 37.2 %ladder.1.l_ref = bf16[768,4096]{1,0:T(8,128)(2,1)} custom-call(s32[16]{0:T(128)} %owner_ref.1, s32[16]{0:T(128)} %convert_reduce_fusion.count_ref, bf16[16,512,128]{2,1,0:T(8,128)(2,1)} %all-gather.2.cloned.1.call-done.f_ref, bf16[16,64,3072]{2,1,0:T(8,128)(2,1)} %spread.1.xt_ref), custom_call_target="tpu_custom_call" | custom-call | flops 40000000000 | bytes 14680064 | tf_op jit(solution)/shard_map/ladder/pallas_call | solution.py:204
  94.5 0.0 collective-permute-done.1
  94.5 13.4 %cycle.1 = bf16[512,4096]{1,0:T(8,128)(2,1)} custom-call(s32[512,1]{1,0:T(8,128)} %fusion.2.slot_col_ref, bf16[768,4096]{1,0:T(8,128)(2,1)} %ladder.1.l_ref, f32[512,4096]{1,0:T(8,128)} %own.1.part_ref, bf16[512,512]{1,0:T(8,128)(2,1)} %get-tuple-element.13.v_ref, bf16[512,4096]{1,0:T(8,128)(2,1)} %bitcast.11.e_ref), custom_call_target="tpu_custom_call" | custom-call | flops 8000000000 | bytes 18874368 | tf_op jit(solution)/shard_map/cycle/pallas_call | solution.py:229
  (4 shorter events, 0.1 us)
Async XLA Ops:
  6.5 7.2 %copy-start = (bf16[64,64]{1,0:T(8,128)(2,1)S(1)}, bf16[64,64]{1,0:T(8,128)(2,1)}, u32[]{:S(2)}) copy-start(bf16[64,64]{1,0:T(8,128)(2,1)} %param.10) | copy-start | bytes 24580
  6.5 6.7 %copy-start.2 = (s32[64,8]{0,1:T(8,128)S(1)}, s32[64,8]{0,1:T(8,128)}, u32[]{:S(2)}) copy-start(s32[64,8]{0,1:T(8,128)} %param.7) | copy-start | bytes 6148
  6.5 7.3 %copy-start.1 = (bf16[64,64]{1,0:T(8,128)(2,1)S(1)}, bf16[64,64]{1,0:T(8,128)(2,1)}, u32[]{:S(2)}) copy-start(bf16[64,64]{1,0:T(8,128)(2,1)} %param.11) | copy-start | bytes 24580
  6.5 50.8 %all-gather.2.cloned.1.call-start = ((), (), s32[]{:S(2)}) async-start(), calls=%async_computation | async-start | bytes 2228224 | tf_op jit(solution)/shard_map/all_gather | solution.py:152
  6.5 24.9 %collective-permute-start = (s32[64,8]{0,1:T(8,128)}, s32[64,8]{0,1:T(8,128)S(1)}, u32[]{:S(2)}, u32[]{:S(2)}) collective-permute-start(s32[64,8]{0,1:T(8,128)} %param.7), channel_id=1, source_target_pairs={{0,1},{1,2},{2,3},{3,4},{4,5},{5,6},{6,7},{7,8},{8,9},{9,10},{10,1... | collective-permute-start | bytes 6152 | tf_op jit(solution)/shard_map/ppermute | solution.py:16
  41.9 52.6 %collective-permute-start.1 = (bf16[64,8,4096]{2,1,0:T(8,128)(2,1)}, bf16[64,8,4096]{2,1,0:T(8,128)(2,1)}, u32[]{:S(2)}, u32[]{:S(2)}) collective-permute-start(bf16[64,8,4096]{2,1,0:T(8,128)(2,1)} %param.6), channel_id=1, source_target_pairs={{0,1},{1,2},{2,3},{3,4},{4,5},{5,6},{6,7},{7,8},{8,9},{9,10},{10,1... | collective-permute-start | bytes 12582920 | tf_op jit(solution)/shard_map/ppermute | solution.py:16
Sparse Core Ops, SparseCore 0:
  13.3 43.9 all-gather.1

commit v3 on v2

--- a/solution.py
+++ b/solution.py
@@ -68,18 +68,27 @@
     pitch = vt + 8
     low = lax.broadcasted_iota(jnp.int32, (half_rows, 128), 1) < 64
     count = count_ref[pl.program_id(0)]
-    row = lax.broadcasted_iota(jnp.int32, (2 * vt, 4 * vt), 0)
-    col = lax.broadcasted_iota(jnp.int32, (2 * vt, 4 * vt), 1)
-    copies = jnp.where(row == vt + col % vt, 1.0, 0.0).astype(BF)
-    tiled = jnp.dot(f_ref[0], copies, preferred_element_type=F32)
-    part = lax.broadcasted_iota(jnp.int32, (vt, 4 * vt), 1) // vt
-    for g in range(naux):
-        for mi in range(4):
-            b_ref[(g * 4 + mi) * vt : (g * 4 + mi + 1) * vt, :] = jnp.where(
-                part == mi, tiled[g * vt : (g + 1) * vt, :], 0.0
-            ).astype(BF)
+    @pl.when(pl.program_id(0) == 0)
+    def _():
+        o_ref[...] = jnp.zeros_like(o_ref)
 
     def run(used):
+        for j in range(pieces):
+            even = o_ref[pl.ds(j, half_rows, stride=pitch), :]
+            odd = o_ref[pl.ds(pieces + j, half_rows, stride=pitch), :]
+            first = jnp.where(low, even, pltpu.roll(odd, 64, 1))
+            second = jnp.where(low, pltpu.roll(even, 64, 1), odd)
+            l_ref[:, j * 128 : (j + 1) * 128] = jnp.concatenate([first, second], 0).astype(BF)
+        row = lax.broadcasted_iota(jnp.int32, (2 * vt, 4 * vt), 0)
+        col = lax.broadcasted_iota(jnp.int32, (2 * vt, 4 * vt), 1)
+        copies = jnp.where(row == vt + col % vt, 1.0, 0.0).astype(BF)
+        tiled = jnp.dot(f_ref[0], copies, preferred_element_type=F32)
+        part = lax.broadcasted_iota(jnp.int32, (vt, 4 * vt), 1) // vt
+        for g in range(naux):
+            for mi in range(4):
+                b_ref[(g * 4 + mi) * vt : (g * 4 + mi + 1) * vt, :] = jnp.where(
+                    part == mi, tiled[g * vt : (g + 1) * vt, :], 0.0
+                ).astype(BF)
         left = f_ref[0, :, :vt]
         for k in range(used):
             half = jnp.dot(
@@ -108,13 +117,6 @@
             fits = jnp.logical_and(fits, count > least)
         pl.when(fits)(functools.partial(run, (turn + 1) * unit))
 
-    for j in range(pieces):
-        even = o_ref[pl.ds(j, half_rows, stride=pitch), :]
-        odd = o_ref[pl.ds(pieces + j, half_rows, stride=pitch), :]
-        first = jnp.where(low, even, pltpu.roll(odd, 64, 1))
-        second = jnp.where(low, pltpu.roll(even, 64, 1), odd)
-        l_ref[:, j * 128 : (j + 1) * 128] = jnp.concatenate([first, second], 0).astype(BF)
-
 
 def own_kernel(w_ref, x_ref, out_ref):
     out_ref[...] = jnp.dot(w_ref[...], x_ref[...], preferred_element_type=F32)
@@ -156,7 +158,7 @@
     ahead = jnp.where(same & (order[:, None] < order[None, :]), 1, 0)
     rank = jnp.sum(ahead, axis=0, dtype=jnp.int32)
     slot = ids * most + rank % 2 * (most // 2) + rank // 2
-    named = ids[:, None] == jnp.arange(tiles, dtype=jnp.int32)[None, :]
+    named = ids[:, None] == jnp.arange(tiles + 1, dtype=jnp.int32)[None, :]
     count = jnp.sum(named, axis=0, dtype=jnp.int32)
     own_weights = spread_weights(cycle_self, ids, ids, listed)
 
@@ -199,19 +201,19 @@
         name="own",
     )(own_weights, x)
 
-    held, columns, own = lax.optimization_barrier((amplitudes, columns, own))
+    held, columns = lax.optimization_barrier((amplitudes, columns))
     earlier = shifted(held, "pair", 1)
     ladder = pl.pallas_call(
         functools.partial(ladder_kernel, most, vt, naux),
         out_shape=jax.ShapeDtypeStruct((slots, width), BF),
         grid_spec=pltpu.PrefetchScalarGridSpec(
             num_scalar_prefetch=2,
-            grid=(tiles,),
+            grid=(tiles + 1,),
             in_specs=[
-                pl.BlockSpec((1, naux * vt, 2 * vt), lambda s, o, n: (o[s], 0, 0)),
-                pl.BlockSpec((1, vt, most * vt), lambda s, o, n: (s, 0, 0)),
+                pl.BlockSpec((1, naux * vt, 2 * vt), lambda s, o, n: (o[jnp.minimum(s, tiles - 1)], 0, 0)),
+                pl.BlockSpec((1, vt, most * vt), lambda s, o, n: (jnp.minimum(s, tiles - 1), 0, 0)),
             ],
-            out_specs=pl.BlockSpec((most, width), lambda s, o, n: (s, 0)),
+            out_specs=pl.BlockSpec((most, width), lambda s, o, n: (jnp.maximum(s - 1, 0), 0)),
             scratch_shapes=[
                 pltpu.VMEM((most // 4 * vt, naux * 256), BF),
                 pltpu.VMEM((naux * 256, 256), BF),
@@ -229,15 +231,15 @@
     residual = pl.pallas_call(
         last_kernel,
         out_shape=jax.ShapeDtypeStruct((items, width), BF),
-        grid=(chunks,),
+        grid=(chunks // 2,),
         in_specs=[
             pl.BlockSpec((items, 1), lambda s: (0, 0)),
-            pl.BlockSpec((slots, wide), lambda s: (0, s)),
-            pl.BlockSpec((items, wide), lambda s: (0, s)),
+            pl.BlockSpec((slots, 2 * wide), lambda s: (0, s)),
+            pl.BlockSpec((items, 2 * wide), lambda s: (0, s)),
             pl.BlockSpec((items, items), lambda s: (0, 0)),
-            pl.BlockSpec((items, wide), lambda s: (0, s)),
-        ],
-        out_specs=pl.BlockSpec((items, wide), lambda s: (0, s)),
+            pl.BlockSpec((items, 2 * wide), lambda s: (0, s)),
+        ],
+        out_specs=pl.BlockSpec((items, 2 * wide), lambda s: (0, s)),
         scratch_shapes=[pltpu.VMEM((items, slots), BF)],
         compiler_params=pltpu.CompilerParams(vmem_limit_bytes=56 * 2**20),
         cost_estimate=pl.CostEstimate(

time: 117 us -> 112 us (0.957); the launches traced: 115 us -> 112 us
  Pallas kernels: 75.7 us -> 70.6 us
  waiting for transfers between devices: 7.11 us -> 9.19 us
    pallas_call x1, Pallas kernels: 37.2 us -> 33.3 us  [shards(): pl.pallas_call(functools.partial(ladder_kernel, most, vt, naux), out_shap...]
    all_gather x1, waiting for transfers between devices: 7.09 us -> 9.16 us  [shards(): everything = lax.all_gather(packed, 'pair', axis=0, tiled=True)]
    pallas_call x1, Pallas kernels: 13.4 us -> 12.1 us  [shards(): pl.pallas_call(last_kernel, out_shape=jax.ShapeDtypeStruct((items, width)...]
  transfers between devices with their start and end apart: 3 -> 3, of which waited for: 1 -> 1; matrix products, arithmetic and copies ran while one was open for 8% -> 8% of each run, Pallas kernels for 54% -> 52%
where the time goes in v3:
time: 112 us
  Pallas kernels  70.6 us (63%)
  between operations  13.5 us (12%)
  waiting for transfers between devices  9.19 us (8%)
  starting transfers between devices  8.96 us (8%)
  local copies, waits for them, and re-layouts  5.69 us (5%)
  other arithmetic  3.74 us (3%)
    pallas_call x1, Pallas kernels, shards(): pl.pallas_call(functools.partial(ladder_kernel, most, vt, naux), out_shap...  33.3 us
    pallas_call x1, Pallas kernels, shards(): pl.pallas_call(functools.partial(spread_kernel, chunks, most, vt), out_sh...  16.2 us
    pallas_call x1, Pallas kernels, shards(): pl.pallas_call(last_kernel, out_shape=jax.ShapeDtypeStruct((items, width)...  12.1 us
    all_gather x1, waiting for transfers between devices, shards(): everything = lax.all_gather(packed, 'pair', axis=0, tiled=True)  9.16 us
    pallas_call x1, Pallas kernels, shards(): pl.pallas_call(own_kernel, out_shape=jax.ShapeDtypeStruct((items, width),...  9.02 us
    ppermute x2, starting transfers between devices, shifted(): lax.ppermute(value, axis, [(source, source + steps) for source in range(f...  8.96 us
  transfers between devices with their start and end apart: 3, of which 1 were waited for; matrix products, arithmetic and copies ran while one was open for 8% of the time, Pallas kernels for 52%

profile of v3, /device:TPU:0, one launch (start us, length us, event | category | flops | bytes accessed | tf_op | source)
XLA Modules:
  0.0 111.7 jit_solution(2932224265630656159)
XLA Ops:
  6.5 0.0 copy-start
  6.5 0.0 copy-start.2
  6.5 0.0 all-gather.2.cloned.1.call-start
  6.5 2.5 %collective-permute-start = (s32[64,8]{0,1:T(8,128)}, s32[64,8]{0,1:T(8,128)S(1)}, u32[]{:S(2)}, u32[]{:S(2)}) collective-permute-start(s32[64,8]{0,1:T(8,128)} %param.7), channel_id=1, source_target_pairs={{0,1},{1,2},{2,3},{3,4},{4,5},{5,6},{6,7},{7,8},{8,9},{9,10},{10,1... | collective-permute-start | bytes 6152 | tf_op jit(solution)/shard_map/ppermute | solution.py:16
  9.0 1.0 fusion.10
  10.0 0.1 copy.89
  10.1 0.1 reshape.210
  10.3 0.5 copy.87
  10.7 1.4 %copy.88 = bf16[1,8,2,32,2,32]{3,2,1,5,4,0:T(2,128)(2,1)S(1)} copy(bf16[1,8,2,32,2,32]{1,4,5,2,3,0:T(2,128)(2,1)S(1)} %bitcast.26) | data formatting | bytes 131072 | tf_op jit(solution)/shard_map/transpose | solution.py:151
  12.1 0.2 reshape.209
  12.4 0.8 copy.90
  13.1 0.0 all-gather.2.cloned.1.call-update
  13.2 0.0 copy-done.2
  13.2 0.1 copy.80
  13.3 0.1 copy.79
  13.4 0.1 mul.55
  13.5 0.1 eq.22
  13.5 0.2 select_reduce_fusion
  13.8 0.6 fusion.9.slot_row_ref
  14.4 0.0 copy-start.1
  14.4 16.2 %spread.1.xt_ref = bf16[16,64,3072]{2,1,0:T(8,128)(2,1)} custom-call(s32[1,512]{1,0:T(1,128)} %fusion.9.slot_row_ref, bf16[512,4096]{1,0:T(8,128)(2,1)} %bitcast.6.x_ref), custom_call_target="tpu_custom_call" | custom-call | flops 24999999488 | bytes 10485760 | tf_op jit(solution)/shard_map/spread/pallas_call | solution.py:165
  30.6 6.5 %collective-permute-start.1 = (bf16[64,8,4096]{2,1,0:T(8,128)(2,1)}, bf16[64,8,4096]{2,1,0:T(8,128)(2,1)}, u32[]{:S(2)}, u32[]{:S(2)}) collective-permute-start(bf16[64,8,4096]{2,1,0:T(8,128)(2,1)} %param.6), channel_id=1, source_target_pairs={{0,1},{1,2},{2,3},{3,4},{4,5},{5,6},{6,7},{7,8},{8,9},{9,10},{10,1... | collective-permute-start | bytes 12582920 | tf_op jit(solution)/shard_map/ppermute | solution.py:16
  37.0 0.1 mul.58
  37.2 0.0 copy-done
  37.2 0.1 copy.92
  37.3 0.0 copy-done.1
  37.3 0.1 copy.95
  37.4 0.2 copy.81
  37.6 0.1 broadcast_bitcast_fusion
  37.7 0.1 broadcast_bitcast_fusion.1
  37.7 1.0 fusion.2.slot_col_ref
  38.7 0.7 convert_reduce_fusion.count_ref
  39.4 0.2 copy.96
  39.6 0.2 copy.93
  39.8 0.0 collective-permute-done
  39.8 0.1 copy.94
  39.9 0.1 eq.29
  40.0 1.3 %compare_select_fusion.1 = (bf16[512,512]{1,0:T(8,128)(2,1)}, bf16[512,512]{1,0:T(8,128)(2,1)}) fusion(bf16[512,512]{1,0:T(8,128)(2,1)S(1)} %copy.96, s32[512]{0:T(512)S(1)} %eq.29, s32[512]{0:T(512)S(1)} %eq.22, bf16[512,512]{1,0:T(8,128)(2,1)S(1)} %copy.93), kind=kLoop, calls=%fused_computation.4 | loop fusion | flops 1048576 | bytes 2101248 | tf_op jit(solution)/shard_map/jit(_where)/select_n | solution.py:21
  41.3 9.0 %own.1.part_ref = f32[512,4096]{1,0:T(8,128)} custom-call(bf16[512,512]{1,0:T(8,128)(2,1)} %get-tuple-element.12.w_ref, bf16[512,4096]{1,0:T(8,128)(2,1)} %bitcast.6.x_ref), custom_call_target="tpu_custom_call" | custom-call | flops 3000000000 | bytes 12582912 | tf_op jit(solution)/shard_map/own/pallas_call | solution.py:188
  50.3 9.2 %all-gather.2.cloned.1.call-done.f_ref = bf16[16,512,128]{2,1,0:T(8,128)(2,1)} async-done(((bf16[1,512,128]{2,1,0:T(8,128)(2,1)}), bf16[16,512,128]{2,1,0:T(8,128)(2,1)}) %all-gather.2.cloned.1.call-update) | async-done | bytes 2097168 | tf_op jit(solution)/shard_map/all_gather | solution.py:154
  59.5 33.3 %ladder.1.l_ref = bf16[768,4096]{1,0:T(8,128)(2,1)} custom-call(s32[16]{0:T(128)} %owner_ref.1, s32[17]{0:T(128)} %convert_reduce_fusion.count_ref, bf16[16,512,128]{2,1,0:T(8,128)(2,1)} %all-gather.2.cloned.1.call-done.f_ref, bf16[16,64,3072]{2,1,0:T(8,128)(2,1)} %spread.1.xt_ref), custom_call_target="tpu_custom_call" | custom-call | flops 40000000000 | bytes 14680064 | tf_op jit(solution)/shard_map/ladder/pallas_call | solution.py:206
  92.8 0.0 collective-permute-done.1
  92.8 12.1 %cycle.1 = bf16[512,4096]{1,0:T(8,128)(2,1)} custom-call(s32[512,1]{1,0:T(8,128)} %fusion.2.slot_col_ref, bf16[768,4096]{1,0:T(8,128)(2,1)} %ladder.1.l_ref, f32[512,4096]{1,0:T(8,128)} %own.1.part_ref, bf16[512,512]{1,0:T(8,128)(2,1)} %get-tuple-element.11.v_ref, bf16[512,4096]{1,0:T(8,128)(2,1)} %bitcast.11.e_ref), custom_call_target="tpu_custom_call" | custom-call | flops 8000000000 | bytes 18874368 | tf_op jit(solution)/shard_map/cycle/pallas_call | solution.py:231
  (4 shorter events, 0.1 us)
Async XLA Ops:
  6.5 30.6 %copy-start = (bf16[64,64]{1,0:T(8,128)(2,1)S(1)}, bf16[64,64]{1,0:T(8,128)(2,1)}, u32[]{:S(2)}) copy-start(bf16[64,64]{1,0:T(8,128)(2,1)} %param.10) | copy-start | bytes 24580
  6.5 6.6 %copy-start.2 = (s32[64,8]{0,1:T(8,128)S(1)}, s32[64,8]{0,1:T(8,128)}, u32[]{:S(2)}) copy-start(s32[64,8]{0,1:T(8,128)} %param.7) | copy-start | bytes 6148
  6.5 52.9 %all-gather.2.cloned.1.call-start = ((), (), s32[]{:S(2)}) async-start(), calls=%async_computation | async-start | bytes 2228224 | tf_op jit(solution)/shard_map/all_gather | solution.py:154
  6.5 33.3 %collective-permute-start = (s32[64,8]{0,1:T(8,128)}, s32[64,8]{0,1:T(8,128)S(1)}, u32[]{:S(2)}, u32[]{:S(2)}) collective-permute-start(s32[64,8]{0,1:T(8,128)} %param.7), channel_id=1, source_target_pairs={{0,1},{1,2},{2,3},{3,4},{4,5},{5,6},{6,7},{7,8},{8,9},{9,10},{10,1... | collective-permute-start | bytes 6152 | tf_op jit(solution)/shard_map/ppermute | solution.py:16
  14.4 22.9 %copy-start.1 = (bf16[64,64]{1,0:T(8,128)(2,1)S(1)}, bf16[64,64]{1,0:T(8,128)(2,1)}, u32[]{:S(2)}) copy-start(bf16[64,64]{1,0:T(8,128)(2,1)} %param.11) | copy-start | bytes 24580
  30.6 62.2 %collective-permute-start.1 = (bf16[64,8,4096]{2,1,0:T(8,128)(2,1)}, bf16[64,8,4096]{2,1,0:T(8,128)(2,1)}, u32[]{:S(2)}, u32[]{:S(2)}) collective-permute-start(bf16[64,8,4096]{2,1,0:T(8,128)(2,1)} %param.6), channel_id=1, source_target_pairs={{0,1},{1,2},{2,3},{3,4},{4,5},{5,6},{6,7},{7,8},{8,9},{9,10},{10,1... | collective-permute-start | bytes 12582920 | tf_op jit(solution)/shard_map/ppermute | solution.py:16
Sparse Core Ops, SparseCore 0:
  13.3 46.1 all-gather.1
